TPU v7x, 512 devices: a whole 4x4x16 slice. The times are simulated.
512 devices in a mesh: wide: 64 (over z_lo, x, core), narrow: 8 (over z_hi, y).
Axes of the slice: x: 4, y: 4, z: 16 (z_hi: 2, z_lo: 8; z = z_hi * 8 + z_lo), core: 2. Of those that a mesh axis runs over, the one named last changes fastest.
Arguments:
- observations: bfloat16 [2048, 8192], P('narrow', 'wide'), may hold values from -6 to 6
- cotangent: bfloat16 [2048, 8192], P('narrow', 'wide'), may hold values from -0.08984375 to 0.08984375
- cell_basis: bfloat16 [8192, 8192], P(None, 'wide'), may hold values from -0.0625 to 0.0625
- cycle_basis: bfloat16 [2048, 2048], P(None, 'narrow'), may hold values from -0.125 to 0.125
- cell_spectrum: float32 [8192], P('wide'), may hold values from 0.05 to 5
- cycle_spectrum: float32 [2048], P('narrow'), may hold values from 0.1 to 4
- noise_var: float32 [1], replicated, may hold values from 0.3 to 1
Outputs:
- coefficients: bfloat16 [2048, 8192], P('narrow', 'wide')
- basis_grad: float32 [2048, 2048], P('wide', 'narrow')
All inputs are finite; a program needn't handle non-finite values.
Results may differ from a plain program's by a relative error of at most 0.0049.
Values may be sent and summed in bfloat16 or wider, within the bound.
A program may use at most 64 MiB of HBM per device.

v0:
```python
import jax
import jax.numpy as jnp
from jax import lax
from jax.sharding import PartitionSpec as P


def contract_first(left, right):
    return lax.dot_general(
        left, right, (((0,), (0,)), ((), ())), preferred_element_type=jnp.float32
    )


def contract_last(left, right):
    return lax.dot_general(
        left, right, (((1,), (1,)), ((), ())), preferred_element_type=jnp.float32
    )


def on_device(
    observations, cotangent, cell_basis, cycle_basis, cell_spectrum, cycle_spectrum, noise_var
):

    def add_cells(block_in):
        return jnp.dot(block_in, cell_basis, preferred_element_type=jnp.float32)

    data_sum = add_cells(lax.all_gather(observations, "wide", axis=1, tiled=True))
    cot_sum = add_cells(lax.all_gather(cotangent, "wide", axis=1, tiled=True))
    proj_data = data_sum.astype(jnp.bfloat16)
    proj_cot = cot_sum.astype(jnp.bfloat16)
    spectrum = cycle_spectrum[:, None] * cell_spectrum[None, :] + noise_var[0]
    full_data, full_cot = (
        lax.all_gather(proj_data, "narrow", axis=0, tiled=True),
        lax.all_gather(proj_cot, "narrow", axis=0, tiled=True),
    )
    rotated = contract_first(cycle_basis, full_data)
    rotated_cot = contract_first(cycle_basis, full_cot)
    coefficients = (rotated / spectrum).astype(jnp.bfloat16)
    scaled_cot = (rotated_cot / spectrum).astype(jnp.bfloat16)
    basis_grad = lax.psum_scatter(
        contract_last(full_cot, coefficients) + contract_last(full_data, scaled_cot),
        "wide",
        scatter_dimension=0,
        tiled=True,
    )
    return (coefficients, basis_grad)


def solution(mesh):
    in_specs = (
        P("narrow", "wide"),
        P("narrow", "wide"),
        P(None, "wide"),
        P(None, "narrow"),
        P("wide"),
        P("narrow"),
        P(),
    )
    out_specs = (P("narrow", "wide"), P("wide", "narrow"))
    return jax.shard_map(
        on_device, mesh=mesh, in_specs=in_specs, out_specs=out_specs, check_vma=False
    )
```

profile of v0, /device:TPU:1, one launch (start us, length us, event | category | flops | bytes accessed | tf_op | source)
XLA Modules:
  0.0 775.2 jit_solution(14725663738183047053)
XLA Ops:
  7.2 0.0 copy-start
  7.2 0.0 all-gather.5.cloned.1.call-start
  7.2 0.7 all-gather.5.cloned.1.call-update
  7.9 0.0 all-gather.3.cloned.1.call-start
  8.0 0.7 all-gather.3.cloned.1.call-update
  8.7 0.0 reduce-scatter.2.cloned.1.call-start
  9.4 132.0 %all-gather.5.cloned.1.call-done = bf16[256,8192]{1,0:T(8,128)(2,1)} async-done(((bf16[256,128]{1,0:T(8,128)(2,1)}), bf16[256,8192]{1,0:T(8,128)(2,1)}) %all-gather.5.cloned.1.call-update) | async-done | bytes 4194320 | tf_op jit(solution)/shard_map/all_gather | solution.py:27
  141.4 0.0 copy-done
  141.4 3.4 convolution_convert_fusion
  144.8 59.5 %all_gather.15 = bf16[2048,128]{1,0:T(8,128)(2,1)S(1)} all-gather(bf16[256,128]{1,0:T(8,128)(2,1)S(1)} %convolution_convert_fusion), channel_id=1, replica_groups=mesh['wide'=64,'narrow'=8] {'narrow'}, dimensions={0}, use_global_device_ids=true | all-gather | bytes 589824 | tf_op jit(solution)/shard_map/all_gather | solution.py:33
  204.3 0.0 copy-start.2
  204.3 0.0 copy-start.3
  204.3 63.9 %all-gather.3.cloned.1.call-done = bf16[256,8192]{1,0:T(8,128)(2,1)} async-done(((bf16[256,128]{1,0:T(8,128)(2,1)}), bf16[256,8192]{1,0:T(8,128)(2,1)}) %all-gather.3.cloned.1.call-update) | async-done | bytes 4194320 | tf_op jit(solution)/shard_map/all_gather | solution.py:26
  268.2 0.0 copy-start.1
  268.2 3.5 convolution_convert_fusion.1
  271.8 58.0 %all_gather.13 = bf16[2048,128]{1,0:T(8,128)(2,1)S(1)} all-gather(bf16[256,128]{1,0:T(8,128)(2,1)S(1)} %convolution_convert_fusion.1), channel_id=1, replica_groups=mesh['wide'=64,'narrow'=8] {'narrow'}, dimensions={0}, use_global_device_ids=true | all-gather | bytes 589824 | tf_op jit(solution)/shard_map/all_gather | solution.py:32
  329.8 0.0 copy-done.2
  329.8 0.0 copy-done.3
  329.8 0.0 copy-done.1
  329.8 0.4 fusion.2
  330.2 1.8 fusion.7
  331.9 4.2 convolution_add_fusion
  336.2 0.0 reduce-scatter.2.cloned.1.call-update
  336.2 0.7 copy.9
  336.9 431.8 %reduce-scatter.2.cloned.1.call-done = f32[32,256]{1,0:T(8,128)} async-done(((f32[2048,256]{1,0:T(8,128)}), f32[32,256]{1,0:T(8,128)}) %reduce-scatter.2.cloned.1.call-update) | async-done | bytes 32784 | tf_op jit(solution)/shard_map/reduce_scatter | solution.py:39
Async XLA Ops:
  7.2 134.2 %copy-start = (bf16[8192,128]{1,0:T(8,128)(2,1)S(1)}, bf16[8192,128]{1,0:T(8,128)(2,1)}, u32[]{:S(2)}) copy-start(bf16[8192,128]{1,0:T(8,128)(2,1)} %param.9) | copy-start | bytes 6291460
  7.2 134.2 %all-gather.5.cloned.1.call-start = ((), (), s32[]{:S(2)}) async-start(), calls=%async_computation.2 | async-start | bytes 4259840 | tf_op jit(solution)/shard_map/all_gather | solution.py:27
  7.9 260.3 %all-gather.3.cloned.1.call-start = ((), (), s32[]{:S(2)}) async-start(), calls=%async_computation.1 | async-start | bytes 4259840 | tf_op jit(solution)/shard_map/all_gather | solution.py:26
  8.7 760.0 %reduce-scatter.2.cloned.1.call-start = ((), (), s32[]{:S(2)}) async-start(), calls=%async_computation.3 | async-start | bytes 2129920 | tf_op jit(solution)/shard_map/reduce_scatter | solution.py:39
  204.3 125.4 %copy-start.2 = (f32[256]{0:T(256)S(1)}, f32[256]{0:T(256)}, u32[]{:S(2)}) copy-start(f32[256]{0:T(256)} %param.12) | copy-start | bytes 3076
  204.3 125.4 %copy-start.3 = (f32[128]{0:T(128)S(1)}, f32[128]{0:T(128)}, u32[]{:S(2)}) copy-start(f32[128]{0:T(128)} %param.11) | copy-start | bytes 1540
  268.2 61.5 %copy-start.1 = (bf16[2048,256]{1,0:T(8,128)(2,1)S(1)}, bf16[2048,256]{1,0:T(8,128)(2,1)}, u32[]{:S(2)}) copy-start(bf16[2048,256]{1,0:T(8,128)(2,1)} %param.10) | copy-start | bytes 3145732
Sparse Core Ops, SparseCore 0:
  10.1 131.2 all-gather.4
  143.5 124.7 all-gather.2
  336.3 432.3 reduce-scatter.1
where the time goes:
time: 785 us; the launch traced here: 775 us
  waiting for transfers between devices  629 us (80%)
  blocking collectives  117 us (15%)
  between operations  14.4 us (2%)
  matrix products  13.3 us (2%)
    reduce_scatter x1, waiting for transfers between devices, on_device(): lax.psum_scatter(contract_last(full_cot, coefficients) + contract_last(fu...  432 us
    all_gather x1, waiting for transfers between devices, on_device(): cot_sum = add_cells(lax.all_gather(cotangent, 'wide', axis=1, tiled=True))  132 us
    all_gather x1, waiting for transfers between devices, on_device(): lax.all_gather(observations, 'wide', axis=1, tiled=True)  63.9 us
    all_gather x1, blocking collectives, on_device(): lax.all_gather(proj_cot, 'narrow', axis=0, tiled=True)  59.5 us
    all_gather x1, blocking collectives, on_device(): lax.all_gather(proj_data, 'narrow', axis=0, tiled=True)  58 us
  transfers between devices with their start and end apart: 3, of which 3 were waited for; matrix products, arithmetic and copies ran while one was open for 1% of the time, Pallas kernels for 0%

commit v1 on v0

v1 whole, which is shorter than its diff:
```python
import jax
import jax.numpy as jnp
from jax import lax
from jax.experimental import pallas as pl
from jax.experimental.pallas import tpu as pltpu
from jax.sharding import PartitionSpec as P

F32 = jnp.float32
BF16 = jnp.bfloat16
MESH = pl.DeviceIdType.MESH


def dot_nt(left, right):
    return lax.dot_general(left, right, (((1,), (1,)), ((), ())), preferred_element_type=F32)


def dot_nn(left, right):
    return lax.dot_general(left, right, (((1,), (0,)), ((), ())), preferred_element_type=F32)


def kernel(
    obs, cot, cb, cyc, cell_row, cyc_row, noise,
    coef_out, grad_out,
    G, W, accO, accS, PS, PF, PB, CT, spec, KO, KS, Q, QS, QR, R, RS, RR,
    cb_sem, z_send, z_recv, x1_send, x1_recv, x2_send, x2_recv,
    ps_sem, h_sem, y_send, y_recv, pb_sem, k_sem, qx_send, qx_recv, rz_send, rz_recv,
):
    w = lax.axis_index("wide")
    n = lax.axis_index("narrow")
    l, x, c = w // 8, (w // 2) % 4, w % 2
    h, y = n // 4, n % 4

    def wide(l_, x_, c_):
        return {"wide": (l_ * 4 + x_) * 2 + c_}

    def narrow(h_, y_):
        return {"narrow": h_ * 4 + y_}

    sib = wide(l, x, 1 - c)
    h_peer = narrow(1 - h, y)
    n_peer = (1 - h) * 4 + y
    x_right, x_left = (x + 1) % 4, (x + 3) % 4

    def rcopy(src, dst, ss, rs, dev):
        return pltpu.make_async_remote_copy(
            src_ref=src, dst_ref=dst, send_sem=ss, recv_sem=rs, device_id=dev, device_id_type=MESH
        )

    bar = pltpu.get_barrier_semaphore()

    def greet(dev):
        pl.semaphore_signal(bar, inc=1, device_id=dev, device_id_type=MESH)

    greet(sib)
    greet(h_peer)
    for d in range(1, 4):
        greet(wide(l, (x + d) % 4, c))
        greet(narrow(h, (y + d) % 4))

    @pl.loop(1, 8)
    def _(k):
        greet(wide((l + k) % 8, x, c))

    G[0, l, x] = obs[...]
    G[1, l, x] = cot[...]
    pl.semaphore_wait(bar, 15)

    def z_copy(t, o, up):
        return rcopy(
            G.at[t, o, x], G.at[t, o, x], z_send.at[t, o, up], z_recv.at[t, o],
            wide(l + 2 * up - 1, x, c),
        )

    def x1_copy(t, o, right):
        to = x_right if right else x_left
        return rcopy(
            G.at[t, o, x], G.at[t, o, x], x1_send.at[t, o, right], x1_recv.at[t, o, right],
            wide(l, to, c),
        )

    def x1_wait(t, o, right):
        frm = x_left if right else x_right
        rcopy(
            G.at[t, o, frm], G.at[t, o, frm], x1_send.at[t, o, right], x1_recv.at[t, o, right],
            wide(l, x_right, c),
        ).wait_recv()

    def x2_copy(t, o):
        right = 1 - o % 2
        frm = (x + 1 + 2 * right) % 4
        to = (x + 3 + 2 * right) % 4
        return rcopy(
            G.at[t, o, frm], G.at[t, o, frm], x2_send.at[t, o], x2_recv.at[t, o], wide(l, to, c)
        )

    def x2_wait(t, o):
        far = (x + 2) % 4
        rcopy(
            G.at[t, o, far], G.at[t, o, far], x2_send.at[t, o], x2_recv.at[t, o],
            wide(l, x_right, c),
        ).wait_recv()

    def x1_start(t, o):
        x1_copy(t, o, 1).start()
        x1_copy(t, o, 0).start()

    def z_step(t, k):
        @pl.when(l >= k)
        def _():
            o = l - k
            z_copy(t, o, 1).wait_recv()

            @pl.when(l < 7)
            def _():
                z_copy(t, o, 1).start()

            x1_start(t, o)

        @pl.when(l + k <= 7)
        def _():
            o = l + k
            z_copy(t, o, 1).wait_recv()

            @pl.when(l > 0)
            def _():
                z_copy(t, o, 0).start()

            x1_start(t, o)

    def x2_one(t, o):
        @pl.when(o % 2 == 0)
        def _():
            x1_wait(t, o, 1)

        @pl.when(o % 2 == 1)
        def _():
            x1_wait(t, o, 0)

        x2_copy(t, o).start()

    def mac(t, o):
        @pl.when(o % 2 == 0)
        def _():
            x1_wait(t, o, 0)

        @pl.when(o % 2 == 1)
        def _():
            x1_wait(t, o, 1)

        x2_wait(t, o)
        s = dot_nn(G[t, o, 0], W[o, 0])
        for xx in range(1, 4):
            s = s + dot_nn(G[t, o, xx], W[o, xx])
        accO[t] += s[:, :128]
        accS[t] += s[:, 128:]

    def both(k, f):
        @pl.when(l >= k)
        def _():
            f(l - k)

        @pl.when(l + k <= 7)
        def _():
            f(l + k)

    for t in range(2):
        @pl.when(l < 7)
        def _():
            z_copy(t, l, 1).start()

        @pl.when(l > 0)
        def _():
            z_copy(t, l, 0).start()

        x1_start(t, l)

    def cb_copy():
        return rcopy(
            cb.at[:, :, 1 - c], W.at[:, :, :, pl.ds(128, 128)], cb_sem.at[0], cb_sem.at[1], sib
        )

    cb_copy().start()

    W[:, :, :, :128] = cb[:, :, c]
    accO[...] = jnp.zeros_like(accO)
    accS[...] = jnp.zeros_like(accS)

    @pl.loop(0, 8)
    def _(i):
        CT[i] = cyc[i].T

    spec[...] = (
        jnp.broadcast_to(cyc_row[...], (128, 256)).T * cell_row[...] + noise[0]
    )

    @pl.loop(1, 8)
    def _(k):
        z_step(0, k)

    x2_one(0, l)

    @pl.loop(1, 8)
    def _(k):
        z_step(1, k)
        both(k, lambda o: x2_one(0, o))

    cb_copy().wait_recv()
    x2_one(1, l)
    mac(0, l)

    @pl.loop(1, 8)
    def _(k):
        both(k, lambda o: x2_one(1, o))
        both(k, lambda o: mac(0, o))

    def ps_copy(t):
        return rcopy(accS.at[t], PS.at[t], ps_sem.at[t, 0], ps_sem.at[t, 1], sib)

    def h_copy(t):
        return rcopy(PF.at[t, n], PF.at[t, n], h_sem.at[t, 0], h_sem.at[t, 1], h_peer)

    def h_wait(t):
        rcopy(
            PF.at[t, n_peer], PF.at[t, n_peer], h_sem.at[t, 0], h_sem.at[t, 1], h_peer
        ).wait_recv()

    def y_copy(t, rel, d):
        m = ((h + rel) % 2) * 4 + y
        return rcopy(
            PF.at[t, m], PF.at[t, m], y_send.at[t, rel, d - 1], y_recv.at[t, rel, d - 1],
            narrow(h, (y + d) % 4),
        )

    def y_wait(t, rel, d):
        m = ((h + rel) % 2) * 4 + (y + 4 - d) % 4
        rcopy(
            PF.at[t, m], PF.at[t, m], y_send.at[t, rel, d - 1], y_recv.at[t, rel, d - 1],
            narrow(h, (y + d) % 4),
        ).wait_recv()

    def finish_proj(t):
        ps_copy(t).wait_recv()
        PF[t, n] = (accO[t] + PS[t]).astype(BF16).reshape(4, 2, 32, 128)
        h_copy(t).start()
        for d in (2, 1, 3):
            y_copy(t, 0, d).start()

    def pass_on(t):
        h_wait(t)
        for d in (2, 1, 3):
            y_copy(t, 1, d).start()

    def pb_copy(t):
        return rcopy(PF.at[t, :, :, 1 - c], PB.at[t], pb_sem.at[t, 0], pb_sem.at[t, 1], sib)

    def rotate(t):
        for rel in range(2):
            for d in range(1, 4):
                y_wait(t, rel, d)
        pb_copy(t).start()
        rot = jnp.zeros((256, 128), F32)
        for m in range(8):
            rot = rot + dot_nn(CT[m], PF[t, m].reshape(256, 128))
        KO[t] = (rot / spec[...]).astype(BF16)
        k_copy(t).start()

    def k_copy(t):
        return rcopy(KO.at[t], KS.at[t], k_sem.at[t, 0], k_sem.at[t, 1], sib)

    ps_copy(0).start()
    mac(1, l)
    finish_proj(0)

    @pl.loop(1, 8)
    def _(k):
        both(k, lambda o: mac(1, o))

    ps_copy(1).start()
    pass_on(0)
    finish_proj(1)
    rotate(0)
    coef_out[...] = KO[0]
    pass_on(1)
    rotate(1)

    for t in range(2):
        pb_copy(t).wait_recv()
        k_copy(t).wait_recv()

    def rows(xx):
        q = dot_nt(PF[1, :, xx, c].reshape(256, 128), KO[0])
        q = q + dot_nt(PF[0, :, xx, c].reshape(256, 128), KO[1])
        q = q + dot_nt(PB[1, :, xx].reshape(256, 128), KS[0])
        q = q + dot_nt(PB[0, :, xx].reshape(256, 128), KS[1])
        return q.reshape(8, 32, 256)

    def qx_copy(d):
        return rcopy(
            QS.at[d - 1], QR.at[d - 1], qx_send.at[d - 1], qx_recv.at[d - 1],
            wide(l, (x + d) % 4, c),
        )

    for d in (2, 1, 3):
        QS[d - 1] = rows((x + d) % 4).astype(BF16)
        qx_copy(d).start()
    Q[...] = rows(x)
    for d in (1, 3, 2):
        qx_copy(d).wait_recv()
    R[...] = Q[...] + QR[0].astype(F32) + QR[2].astype(F32) + QR[1].astype(F32)
    RS[...] = R[...].astype(BF16)

    def rz_copy(k):
        to = (l + k) % 8
        return rcopy(RS.at[to], RR.at[l], rz_send.at[k], rz_recv.at[l], wide(to, x, c))

    def rz_wait(k):
        frm = (l + k) % 8
        rcopy(RR.at[frm], RR.at[frm], rz_send.at[k], rz_recv.at[frm], wide(frm, x, c)).wait_recv()

    @pl.loop(1, 8)
    def _(k):
        rz_copy(k).start()

    grad_out[...] = R[l]

    @pl.loop(1, 8)
    def _(k):
        rz_wait(k)
        grad_out[...] += RR[(l + k) % 8].astype(F32)

    cb_copy().wait_send()
    for t in range(2):
        @pl.loop(0, 8)
        def _(o):
            @pl.when(jnp.logical_and(o <= l, l < 7))
            def _():
                z_copy(t, o, 1).wait_send()

            @pl.when(jnp.logical_and(o >= l, l > 0))
            def _():
                z_copy(t, o, 0).wait_send()

            x1_copy(t, o, 1).wait_send()
            x1_copy(t, o, 0).wait_send()
            x2_copy(t, o).wait_send()

        ps_copy(t).wait_send()
        h_copy(t).wait_send()
        for rel in range(2):
            for d in range(1, 4):
                y_copy(t, rel, d).wait_send()
        pb_copy(t).wait_send()
        k_copy(t).wait_send()
    for d in range(1, 4):
        qx_copy(d).wait_send()

    @pl.loop(1, 8)
    def _(k):
        rz_copy(k).wait_send()


def on_device(obs, cot, cell_basis, cycle_basis, cell_spectrum, cycle_spectrum, noise_var):
    vmem = pl.BlockSpec(memory_space=pltpu.VMEM)
    dma = pltpu.SemaphoreType.DMA
    return pl.pallas_call(
        kernel,
        out_shape=(
            jax.ShapeDtypeStruct((256, 128), BF16),
            jax.ShapeDtypeStruct((32, 256), F32),
        ),
        in_specs=[vmem] * 6 + [pl.BlockSpec(memory_space=pltpu.SMEM)],
        out_specs=(vmem, vmem),
        scratch_shapes=[
            pltpu.VMEM((2, 8, 4, 256, 128), BF16),
            pltpu.VMEM((8, 4, 128, 256), BF16),
            pltpu.VMEM((2, 256, 128), F32),
            pltpu.VMEM((2, 256, 128), F32),
            pltpu.VMEM((2, 256, 128), F32),
            pltpu.VMEM((2, 8, 4, 2, 32, 128), BF16),
            pltpu.VMEM((2, 8, 4, 32, 128), BF16),
            pltpu.VMEM((8, 256, 256), BF16),
            pltpu.VMEM((256, 128), F32),
            pltpu.VMEM((2, 256, 128), BF16),
            pltpu.VMEM((2, 256, 128), BF16),
            pltpu.VMEM((8, 32, 256), F32),
            pltpu.VMEM((3, 8, 32, 256), BF16),
            pltpu.VMEM((3, 8, 32, 256), BF16),
            pltpu.VMEM((8, 32, 256), F32),
            pltpu.VMEM((8, 32, 256), BF16),
            pltpu.VMEM((8, 32, 256), BF16),
            dma((2,)),
            dma((2, 8, 2)), dma((2, 8)),
            dma((2, 8, 2)), dma((2, 8, 2)),
            dma((2, 8)), dma((2, 8)),
            dma((2, 2)), dma((2, 2)),
            dma((2, 2, 3)), dma((2, 2, 3)),
            dma((2, 2)), dma((2, 2)),
            dma((3,)), dma((3,)),
            dma((8,)), dma((8,)),
        ],
        compiler_params=pltpu.CompilerParams(
            collective_id=0, has_side_effects=True, vmem_limit_bytes=48 << 20
        ),
    )(
        obs,
        cot,
        cell_basis.reshape(8, 4, 2, 128, 128),
        cycle_basis.reshape(8, 256, 256),
        cell_spectrum.reshape(1, 128),
        cycle_spectrum.reshape(1, 256),
        noise_var,
    )


def solution(mesh):
    in_specs = (
        P("narrow", "wide"),
        P("narrow", "wide"),
        P(None, "wide"),
        P(None, "narrow"),
        P("wide"),
        P("narrow"),
        P(),
    )
    out_specs = (P("narrow", "wide"), P("wide", "narrow"))
    return jax.shard_map(
        on_device, mesh=mesh, in_specs=in_specs, out_specs=out_specs, check_vma=False
    )
```

time: 785 us -> 113 us (0.14); the launches traced: 775 us -> 112 us
  waiting for transfers between devices: 629 us -> 0 us
  blocking collectives: 117 us -> 0 us
  Pallas kernels: 0 us -> 104 us
  matrix products: 13.3 us -> 0 us
  between operations: 14.4 us -> 1.3 us
    reduce_scatter x1 -> x0, waiting for transfers between devices: 432 us -> none  [on_device(): lax.psum_scatter(contract_last(full_cot, coefficients) + contract_last(fu...]
    all_gather x2 -> x0, waiting for transfers between devices: 196 us -> none  [the longest x1 132 us: on_device(): cot_sum = add_cells(lax.all_gather(cotangent, 'wide', axis=1, tiled=True))]
    all_gather x2 -> x0, blocking collectives: 117 us -> none  [the longest x1 59.5 us: on_device(): lax.all_gather(proj_cot, 'narrow', axis=0, tiled=True)]
    pallas_call x0 -> x1, Pallas kernels: none -> 104 us  [on_device(): pl.pallas_call(kernel, out_shape=(jax.ShapeDtypeStruct((256, 128), BF16),...]
    dot_general x5 -> x0, matrix products: 13.3 us -> none  [the longest x2 6.94 us: add_cells(): return jnp.dot(block_in, cell_basis, preferred_element_type=jnp.float32)]
  transfers between devices with their start and end apart: 3 -> 0, of which waited for: 3 -> 0; matrix products, arithmetic and copies ran while one was open for 1% -> 0% of each run, Pallas kernels for 0% -> 0%
where the time goes in v1:
time: 113 us; the launch traced here: 112 us
  Pallas kernels  104 us (92%)
  local copies, waits for them, and re-layouts  7.07 us (6%)
  between operations  1.3 us (1%)
    pallas_call x1, Pallas kernels, on_device(): pl.pallas_call(kernel, out_shape=(jax.ShapeDtypeStruct((256, 128), BF16),...  104 us
    unnamed x14, local copies, waits for them, and re-layouts  7.07 us

profile of v1, /device:TPU:1, one launch (start us, length us, event | category | flops | bytes accessed | tf_op | source)
XLA Modules:
  0.0 112.5 jit_solution(10254503754610729837)
XLA Ops:
  1.3 0.0 copy-start
  1.3 1.6 %copy-done = bf16[8192,128]{1,0:T(8,128)(2,1)S(1)} copy-done((bf16[8192,128]{1,0:T(8,128)(2,1)S(1)}, bf16[8192,128]{1,0:T(8,128)(2,1)}, u32[]{:S(2)}) %copy-start) | copy-done | bytes 2097176
  2.9 0.0 copy-start.1
  2.9 1.2 %copy-done.1 = bf16[2048,256]{1,0:T(8,128)(2,1)S(1)} copy-done((bf16[2048,256]{1,0:T(8,128)(2,1)S(1)}, bf16[2048,256]{1,0:T(8,128)(2,1)}, u32[]{:S(2)}) %copy-start.1) | copy-done | bytes 1048600
  4.1 0.0 copy-start.2
  4.1 0.8 copy-done.2
  4.9 0.0 copy-start.3
  4.9 0.8 copy-done.3
  5.8 0.0 copy-start.4
  5.8 0.7 copy-done.4
  6.5 0.0 copy-start.5
  6.5 0.7 copy-done.5
  7.1 104.1 %shard_map.86 = (bf16[256,128]{1,0:T(8,128)(2,1)S(1)}, f32[32,256]{1,0:T(8,128)S(1)}) custom-call(bf16[256,128]{1,0:T(8,128)(2,1)S(1)} %copy-done.2, bf16[256,128]{1,0:T(8,128)(2,1)S(1)} %copy-done.3, bf16[8,4,2,128,128]{4,3,2,1,0:T(8,128)(2,1)S(1)} %bitcast.4, bf16[8,256,256]{2,1,0:T(8,128)(2,1)S(1)} %bitcast.5, f32[1,128]{1,0:T(1,128)S(1)} %bitcast.7, ...), custom_call_target="tpu_custom_call" | custom-call | tf_op jit(solution)/shard_map/pallas_call | solution.py:365
  111.2 0.6 copy.12
  111.9 0.6 copy.13
Async XLA Ops:
  1.3 1.6 %copy-start = (bf16[8192,128]{1,0:T(8,128)(2,1)S(1)}, bf16[8192,128]{1,0:T(8,128)(2,1)}, u32[]{:S(2)}) copy-start(bf16[8192,128]{1,0:T(8,128)(2,1)} %param.9) | copy-start | bytes 6291460
  2.9 1.2 %copy-start.1 = (bf16[2048,256]{1,0:T(8,128)(2,1)S(1)}, bf16[2048,256]{1,0:T(8,128)(2,1)}, u32[]{:S(2)}) copy-start(bf16[2048,256]{1,0:T(8,128)(2,1)} %param.10) | copy-start | bytes 3145732
  4.1 0.8 copy-start.2
  4.9 0.8 copy-start.3
  5.8 0.7 copy-start.4
  6.5 0.7 copy-start.5

commit v2 on v1

v2 whole, which is shorter than its diff:
```python
import jax
import jax.numpy as jnp
from jax import lax
from jax.experimental import pallas as pl
from jax.experimental.pallas import tpu as pltpu
from jax.sharding import PartitionSpec as P

F32 = jnp.float32
BF16 = jnp.bfloat16
MESH = pl.DeviceIdType.MESH


def dot_nt(left, right):
    return lax.dot_general(left, right, (((1,), (1,)), ((), ())), preferred_element_type=F32)


def dot_nn(left, right):
    return lax.dot_general(left, right, (((1,), (0,)), ((), ())), preferred_element_type=F32)


def kernel(
    obs, cot, cb, cyc, cell_row, cyc_row, noise,
    coef_out, grad_out,
    G, W, acc, XS, XR, PF, PB, cycV, CT, cellV, cycrV, noiseV, spec, KO, KS,
    Q, QS, QR, R, RS, RR,
    in_sem, z_send, zj_send, z_recv, g_send, g_recv,
    wx_send, wx_recv, wy_send, wy_recv, xr_send, xr_recv,
    h_sem, y_send, y_recv, pb_sem, k_sem, qx_send, qx_recv, rz_send, rz_recv,
):
    w = lax.axis_index("wide")
    n = lax.axis_index("narrow")
    l, x, c = w // 8, (w // 2) % 4, w % 2
    h, y = n // 4, n % 4

    def wide(l_, x_, c_):
        return {"wide": (l_ * 4 + x_) * 2 + c_}

    def narrow(h_, y_):
        return {"narrow": h_ * 4 + y_}

    sib = wide(l, x, 1 - c)
    h_peer = narrow(1 - h, y)
    n_peer = (1 - h) * 4 + y

    def rcopy(src, dst, ss, rs, dev):
        return pltpu.make_async_remote_copy(
            src_ref=src, dst_ref=dst, send_sem=ss, recv_sem=rs, device_id=dev, device_id_type=MESH
        )

    bar = pltpu.get_barrier_semaphore()

    def greet(dev):
        pl.semaphore_signal(bar, inc=1, device_id=dev, device_id_type=MESH)

    greet(h_peer)

    @pl.loop(1, 8)
    def _(k):
        greet(wide((l + k) % 8, x, c))

    for d in range(1, 4):
        greet(wide(l, (x + d) % 4, c))
        greet(narrow(h, (y + d) % 4))
    greet(sib)

    loads = [
        pltpu.make_async_copy(obs, G.at[0, l, c], in_sem.at[0]),
        pltpu.make_async_copy(cot, G.at[1, l, c], in_sem.at[1]),
        pltpu.make_async_copy(cb.at[:, x], W.at[:, :, :, pl.ds(0, 128)], in_sem.at[2]),
        pltpu.make_async_copy(cyc, cycV, in_sem.at[3]),
        pltpu.make_async_copy(cell_row, cellV, in_sem.at[4]),
        pltpu.make_async_copy(cyc_row, cycrV, in_sem.at[5]),
        pltpu.make_async_copy(noise, noiseV, in_sem.at[6]),
    ]
    for load in loads:
        load.start()
    loads[0].wait()
    loads[1].wait()
    pl.semaphore_wait(bar, 15)

    def z_copy(t, o, up):
        return rcopy(
            G.at[t, o, c], G.at[t, o, c], z_send.at[t, o, up], z_recv.at[t, o],
            wide(l + 2 * up - 1, x, c),
        )

    def z_jump(t, up):
        return rcopy(
            G.at[t, l, c], G.at[t, l, c], zj_send.at[t, up], z_recv.at[t, l],
            wide(l + 8 * up - 4, x, c),
        )

    def g_copy(t, o):
        return rcopy(G.at[t, o, c], G.at[t, o, c], g_send.at[t, o], g_recv.at[t, o], sib)

    def g_wait(t, o):
        rcopy(
            G.at[t, o, 1 - c], G.at[t, o, 1 - c], g_send.at[t, o], g_recv.at[t, o], sib
        ).wait_recv()

    def z_step(t, k):
        @pl.when(l >= k)
        def _():
            o = l - k
            z_copy(t, o, 1).wait_recv()
            if k != 3:
                @pl.when(l < 7)
                def _():
                    z_copy(t, o, 1).start()

            g_copy(t, o).start()

        @pl.when(l + k <= 7)
        def _():
            o = l + k
            z_copy(t, o, 1).wait_recv()
            if k != 3:
                @pl.when(l > 0)
                def _():
                    z_copy(t, o, 0).start()

            g_copy(t, o).start()

    def wx_copy(d, p):
        q = (y + 2 * p) % 4
        to = (x + d) % 4
        return rcopy(
            cb.at[pl.ds(2 * q, 2), to],
            W.at[pl.ds(2 * q, 2), :, :, pl.ds(128 * (4 - d), 128)],
            wx_send.at[d - 1, p], wx_recv.at[d - 1, p], wide(l, to, c),
        )

    def wx_wait(d, p):
        q = (y + 2 * p) % 4
        part = W.at[pl.ds(2 * q, 2), :, :, pl.ds(128 * (4 - d), 128)]
        rcopy(part, part, wx_send.at[d - 1, p], wx_recv.at[d - 1, p], sib).wait_recv()

    def wy_copy(d, up):
        part = W.at[pl.ds(2 * y, 2), :, :, pl.ds(128 * (4 - d), 128)]
        return rcopy(
            part, part, wy_send.at[d - 1, up], wy_recv.at[d - 1, up],
            narrow(h, (y + 2 * up + 3) % 4),
        )

    def wy_wait(d, up):
        q = (y + 5 - 2 * up) % 4
        part = W.at[pl.ds(2 * q, 2), :, :, pl.ds(128 * (4 - d), 128)]
        rcopy(part, part, wy_send.at[d - 1, up], wy_recv.at[d - 1, up], sib).wait_recv()

    def w_step(d):
        wx_wait(d, 0)
        wy_copy(d, 1).start()
        wy_copy(d, 0).start()

    for t in range(2):
        @pl.when(l < 7)
        def _():
            z_copy(t, l, 1).start()

        @pl.when(l > 0)
        def _():
            z_copy(t, l, 0).start()

        @pl.when(l < 4)
        def _():
            z_jump(t, 1).start()

        @pl.when(l >= 4)
        def _():
            z_jump(t, 0).start()

        if t == 0:
            for d in (1, 3, 2):
                wx_copy(d, 0).start()
        g_copy(t, l).start()
    for d in (1, 3, 2):
        wx_copy(d, 1).start()

    for i in range(3, 7):
        loads[i].wait()

    @pl.loop(0, 8)
    def _(i):
        CT[i] = cycV[i].T

    spec[...] = jnp.broadcast_to(cycrV[...], (128, 256)).T * cellV[...] + noiseV[...]

    for t, k in ((0, 1), (0, 4), (1, 1), (0, 2), (1, 4)):
        z_step(t, k)
    w_step(1)
    w_step(3)
    for t, k in ((0, 5), (1, 2), (0, 3)):
        z_step(t, k)
    w_step(2)
    for t, k in ((1, 5), (0, 6), (1, 3), (0, 7), (1, 6)):
        z_step(t, k)

    loads[2].wait()
    for d in (1, 3, 2):
        wx_wait(d, 1)
        wy_wait(d, 0)
        wy_wait(d, 1)

    def mac(t, o):
        g_wait(t, o)
        block = jnp.concatenate([G[t, o, 0], G[t, o, 1]], axis=1)
        acc[t] += dot_nn(block, W[o].reshape(256, 512))

    def xr_copy(t, d):
        return rcopy(
            XS.at[t, d - 1], XR.at[t, d - 1], xr_send.at[t, d - 1], xr_recv.at[t, d - 1],
            wide(l, (x + d) % 4, c),
        )

    def send_partials(t):
        for d in (2, 1, 3):
            XS[t, d - 1] = acc[t, :, 128 * d : 128 * d + 128].astype(BF16)
            xr_copy(t, d).start()

    acc[...] = jnp.zeros_like(acc)

    @pl.loop(0, 8)
    def _(o):
        mac(0, o)

    send_partials(0)

    z_step(1, 7)
    mac(1, l)

    @pl.loop(1, 8)
    def _(k):
        mac(1, (l + k) % 8)

    send_partials(1)

    def h_copy(t):
        return rcopy(PF.at[t, n], PF.at[t, n], h_sem.at[t, 0], h_sem.at[t, 1], h_peer)

    def h_wait(t):
        rcopy(
            PF.at[t, n_peer], PF.at[t, n_peer], h_sem.at[t, 0], h_sem.at[t, 1], h_peer
        ).wait_recv()

    def y_copy(t, rel, d):
        m = ((h + rel) % 2) * 4 + y
        return rcopy(
            PF.at[t, m], PF.at[t, m], y_send.at[t, rel, d - 1], y_recv.at[t, rel, d - 1],
            narrow(h, (y + d) % 4),
        )

    def y_wait(t, rel, d):
        m = ((h + rel) % 2) * 4 + (y + 4 - d) % 4
        rcopy(
            PF.at[t, m], PF.at[t, m], y_send.at[t, rel, d - 1], y_recv.at[t, rel, d - 1],
            narrow(h, (y + d) % 4),
        ).wait_recv()

    def finish_proj(t):
        total = acc[t, :, :128]
        for d in (1, 3, 2):
            xr_copy(t, d).wait_recv()
            total = total + XR[t, d - 1].astype(F32)
        PF[t, n] = total.astype(BF16).reshape(4, 2, 32, 128)
        h_copy(t).start()
        for d in (2, 1, 3):
            y_copy(t, 0, d).start()

    def pass_on(t):
        h_wait(t)
        for d in (2, 1, 3):
            y_copy(t, 1, d).start()

    def pb_copy(t):
        return rcopy(PF.at[t, :, :, 1 - c], PB.at[t], pb_sem.at[t, 0], pb_sem.at[t, 1], sib)

    def k_copy(t):
        return rcopy(KO.at[t], KS.at[t], k_sem.at[t, 0], k_sem.at[t, 1], sib)

    def rotate(t):
        for rel in range(2):
            for d in range(1, 4):
                y_wait(t, rel, d)
        pb_copy(t).start()
        rot = jnp.zeros((256, 128), F32)
        for m in range(8):
            rot = rot + dot_nn(CT[m], PF[t, m].reshape(256, 128))
        KO[t] = (rot / spec[...]).astype(BF16)
        k_copy(t).start()

    finish_proj(0)
    finish_proj(1)
    pass_on(0)
    rotate(0)
    coef_out[...] = KO[0]
    pass_on(1)
    rotate(1)

    for t in range(2):
        pb_copy(t).wait_recv()
        k_copy(t).wait_recv()

    def rows(xx):
        q = dot_nt(PF[1, :, xx, c].reshape(256, 128), KO[0])
        q = q + dot_nt(PF[0, :, xx, c].reshape(256, 128), KO[1])
        q = q + dot_nt(PB[1, :, xx].reshape(256, 128), KS[0])
        q = q + dot_nt(PB[0, :, xx].reshape(256, 128), KS[1])
        return q.reshape(8, 32, 256)

    def qx_copy(d):
        return rcopy(
            QS.at[d - 1], QR.at[d - 1], qx_send.at[d - 1], qx_recv.at[d - 1],
            wide(l, (x + d) % 4, c),
        )

    for d in (2, 1, 3):
        QS[d - 1] = rows((x + d) % 4).astype(BF16)
        qx_copy(d).start()
    Q[...] = rows(x)
    for d in (1, 3, 2):
        qx_copy(d).wait_recv()
    R[...] = Q[...] + QR[0].astype(F32) + QR[2].astype(F32) + QR[1].astype(F32)
    RS[...] = R[...].astype(BF16)

    def rz_copy(k):
        to = (l + k) % 8
        return rcopy(RS.at[to], RR.at[l], rz_send.at[k], rz_recv.at[l], wide(to, x, c))

    def rz_wait(k):
        frm = (l + k) % 8
        rcopy(RR.at[frm], RR.at[frm], rz_send.at[k], rz_recv.at[frm], wide(frm, x, c)).wait_recv()

    @pl.loop(1, 8)
    def _(k):
        rz_copy(k).start()

    grad_out[...] = R[l]

    @pl.loop(1, 8)
    def _(k):
        rz_wait(k)
        grad_out[...] += RR[(l + k) % 8].astype(F32)

    def drain_gather():
        for t in range(2):
            @pl.loop(0, 8)
            def _(o):
                @pl.when(jnp.logical_and(jnp.logical_and(o <= l, l < 7), l - o != 3))
                def _():
                    z_copy(t, o, 1).wait_send()

                @pl.when(jnp.logical_and(jnp.logical_and(o >= l, l > 0), o - l != 3))
                def _():
                    z_copy(t, o, 0).wait_send()

                g_copy(t, o).wait_send()

            @pl.when(l < 4)
            def _():
                z_jump(t, 1).wait_send()

            @pl.when(l >= 4)
            def _():
                z_jump(t, 0).wait_send()

            for d in range(1, 4):
                wx_copy(d, t).wait_send()
                wy_copy(d, t).wait_send()

    def drain_partials():
        for t in range(2):
            for d in range(1, 4):
                xr_copy(t, d).wait_send()

    def drain_proj():
        for t in range(2):
            h_copy(t).wait_send()
            for rel in range(2):
                for d in range(1, 4):
                    y_copy(t, rel, d).wait_send()
            pb_copy(t).wait_send()
            k_copy(t).wait_send()

    drain_gather()
    drain_partials()
    drain_proj()
    for d in range(1, 4):
        qx_copy(d).wait_send()

    @pl.loop(1, 8)
    def _(k):
        rz_copy(k).wait_send()


def on_device(obs, cot, cell_basis, cycle_basis, cell_spectrum, cycle_spectrum, noise_var):
    vmem = pl.BlockSpec(memory_space=pltpu.VMEM)
    dma = pltpu.SemaphoreType.DMA
    return pl.pallas_call(
        kernel,
        out_shape=(
            jax.ShapeDtypeStruct((256, 128), BF16),
            jax.ShapeDtypeStruct((32, 256), F32),
        ),
        in_specs=[pl.BlockSpec(memory_space=pltpu.HBM)] * 7,
        out_specs=(vmem, vmem),
        scratch_shapes=[
            pltpu.VMEM((2, 8, 2, 256, 128), BF16),
            pltpu.VMEM((8, 2, 128, 512), BF16),
            pltpu.VMEM((2, 256, 512), F32),
            pltpu.VMEM((2, 3, 256, 128), BF16),
            pltpu.VMEM((2, 3, 256, 128), BF16),
            pltpu.VMEM((2, 8, 4, 2, 32, 128), BF16),
            pltpu.VMEM((2, 8, 4, 32, 128), BF16),
            pltpu.VMEM((8, 256, 256), BF16),
            pltpu.VMEM((8, 256, 256), BF16),
            pltpu.VMEM((1, 128), F32),
            pltpu.VMEM((1, 256), F32),
            pltpu.VMEM((1, 1), F32),
            pltpu.VMEM((256, 128), F32),
            pltpu.VMEM((2, 256, 128), BF16),
            pltpu.VMEM((2, 256, 128), BF16),
            pltpu.VMEM((8, 32, 256), F32),
            pltpu.VMEM((3, 8, 32, 256), BF16),
            pltpu.VMEM((3, 8, 32, 256), BF16),
            pltpu.VMEM((8, 32, 256), F32),
            pltpu.VMEM((8, 32, 256), BF16),
            pltpu.VMEM((8, 32, 256), BF16),
            dma((7,)),
            dma((2, 8, 2)), dma((2, 2)), dma((2, 8)),
            dma((2, 8)), dma((2, 8)),
            dma((3, 2)), dma((3, 2)),
            dma((3, 2)), dma((3, 2)),
            dma((2, 3)), dma((2, 3)),
            dma((2, 2)),
            dma((2, 2, 3)), dma((2, 2, 3)),
            dma((2, 2)), dma((2, 2)),
            dma((3,)), dma((3,)),
            dma((8,)), dma((8,)),
        ],
        compiler_params=pltpu.CompilerParams(
            collective_id=0, has_side_effects=True, vmem_limit_bytes=60 << 20
        ),
    )(
        obs,
        cot,
        cell_basis.reshape(8, 4, 2, 128, 128),
        cycle_basis.reshape(8, 256, 256),
        cell_spectrum.reshape(1, 128),
        cycle_spectrum.reshape(1, 256),
        noise_var.reshape(1, 1),
    )


def solution(mesh):
    in_specs = (
        P("narrow", "wide"),
        P("narrow", "wide"),
        P(None, "wide"),
        P(None, "narrow"),
        P("wide"),
        P("narrow"),
        P(),
    )
    out_specs = (P("narrow", "wide"), P("wide", "narrow"))
    return jax.shard_map(
        on_device, mesh=mesh, in_specs=in_specs, out_specs=out_specs, check_vma=False
    )
```

time: 113 us -> 95.4 us (0.84)
  Pallas kernels: 104 us -> 91 us
  local copies, waits for them, and re-layouts: 7.07 us -> 2.85 us
    pallas_call x1, Pallas kernels: 104 us -> 91 us  [on_device(): pl.pallas_call(kernel, out_shape=(jax.ShapeDtypeStruct((256, 128), BF16),...]
    unnamed x14 -> x2, local copies, waits for them, and re-layouts: 7.07 us -> 2.85 us
where the time goes in v2:
time: 95.4 us; the launch traced here: 95.1 us
  Pallas kernels  91 us (95%)
  local copies, waits for them, and re-layouts  2.85 us (3%)
  between operations  1.29 us (1%)
    pallas_call x1, Pallas kernels, on_device(): pl.pallas_call(kernel, out_shape=(jax.ShapeDtypeStruct((256, 128), BF16),...  91 us
    unnamed x2, local copies, waits for them, and re-layouts  2.85 us

profile of v2, /device:TPU:1, one launch (start us, length us, event | category | flops | bytes accessed | tf_op | source)
XLA Modules:
  0.0 95.1 jit_solution(9691741813940936183)
XLA Ops:
  1.3 91.0 %shard_map.86 = (bf16[256,128]{1,0:T(8,128)(2,1)}, f32[32,256]{1,0:T(8,128)}) custom-call(bf16[256,128]{1,0:T(8,128)(2,1)} %obs.1, bf16[256,128]{1,0:T(8,128)(2,1)} %cot.1, bf16[8,4,2,128,128]{4,3,2,1,0:T(8,128)(2,1)} %bitcast.6, bf16[8,256,256]{2,1,0:T(8,128)(2,1)} %bitcast.7, f32[1,128]{1,0:T(1,128)} %bitcast.9, f32[1,256]{1,0:T(1,128)} %bitcast.8, ...), custom_call_target="tpu_custom_call" | custom-call | tf_op jit(solution)/shard_map/pallas_call | solution.py:398
  92.3 1.5 %copy.12 = bf16[256,128]{1,0:T(8,128)(2,1)} copy(bf16[256,128]{1,0:T(8,128)(2,1)} %get-tuple-element.4) | data formatting | bytes 131072
  93.8 1.4 %copy.13 = f32[32,256]{1,0:T(8,128)} copy(f32[32,256]{1,0:T(8,128)} %get-tuple-element.5) | data formatting | bytes 65536

commit v3 on v2

v3 whole, which is shorter than its diff:
```python
import jax
import jax.numpy as jnp
from jax import lax
from jax.experimental import pallas as pl
from jax.experimental.pallas import tpu as pltpu
from jax.sharding import PartitionSpec as P

F32 = jnp.float32
BF16 = jnp.bfloat16
MESH = pl.DeviceIdType.MESH


def dot_nt(left, right):
    return lax.dot_general(left, right, (((1,), (1,)), ((), ())), preferred_element_type=F32)


def dot_nn(left, right):
    return lax.dot_general(left, right, (((1,), (0,)), ((), ())), preferred_element_type=F32)


def kernel(
    obs, cot, cb, cyc, cell_row, cyc_row, noise,
    coef_out, grad_out,
    G, W, acc, XS, XR, PF, PB, cycV, CT, cellV, cycrV, noiseS, spec, KO, KS,
    Q, QS, QR, R, RS, RR,
    in_sem, g0_sem, z_send, z_recv, g_send, g_recv,
    wx_send, wx_recv, wy_send, wy_recv, xr_send, xr_recv,
    y_send, y_recv, pb_sem, k_sem, qx_send, qx_recv, rz_send, rz_recv,
):
    w = lax.axis_index("wide")
    n = lax.axis_index("narrow")
    l, x, c = w // 8, (w // 2) % 4, w % 2
    h, y = n // 4, n % 4
    z = h * 8 + l
    s = 1 - 2 * c

    def wide(l_, x_, c_):
        return {"wide": (l_ * 4 + x_) * 2 + c_}

    def narrow(h_, y_):
        return {"narrow": h_ * 4 + y_}

    def along_z(z_):
        return {"wide": ((z_ % 8) * 4 + x) * 2 + c, "narrow": (z_ // 8) * 4 + y}

    sib = wide(l, x, 1 - c)

    def rcopy(src, dst, ss, rs, dev):
        return pltpu.make_async_remote_copy(
            src_ref=src, dst_ref=dst, send_sem=ss, recv_sem=rs, device_id=dev, device_id_type=MESH
        )

    bar = pltpu.get_barrier_semaphore()

    def greet(dev):
        pl.semaphore_signal(bar, inc=1, device_id=dev, device_id_type=MESH)

    for d in (2, 1, 3):
        greet(wide(l, (x + d) % 4, c))
        greet(narrow(h, (y + d) % 4))
    greet(along_z((z - 2 * s + 16) % 16))
    greet(along_z((z - s + 16) % 16))
    greet(sib)

    loads = [
        pltpu.make_async_copy(obs, G.at[0, z, c], in_sem.at[0]),
        pltpu.make_async_copy(cot, G.at[1, z, c], in_sem.at[1]),
        pltpu.make_async_copy(cb.at[:, x], W.at[:, :, :, pl.ds(0, 128)], in_sem.at[2]),
        pltpu.make_async_copy(cyc, cycV, in_sem.at[3]),
        pltpu.make_async_copy(cell_row, cellV, in_sem.at[4]),
        pltpu.make_async_copy(cyc_row, cycrV, in_sem.at[5]),
        pltpu.make_async_copy(noise, noiseS, in_sem.at[6]),
    ]
    for load in loads:
        load.start()
    loads[0].wait()
    loads[1].wait()
    pl.semaphore_wait(bar, 9)

    def z_copy(t, o, q, hop=1):
        part = G.at[t, o, q]
        return rcopy(
            part, part, z_send.at[t, o, q, hop - 1], z_recv.at[t, o, q],
            along_z((z + hop * s + 16) % 16),
        )

    def g0_copy(t):
        return rcopy(G.at[t, z, c], G.at[t, z, c], g0_sem.at[t, 0], g0_sem.at[t, 1], sib)

    def g0_wait(t):
        part = G.at[t, z, 1 - c]
        rcopy(part, part, g0_sem.at[t, 0], g0_sem.at[t, 1], sib).wait_recv()

    def g_copy(t, o):
        return rcopy(G.at[t, o], G.at[t, o], g_send.at[t, o], g_recv.at[t, o], sib)

    def origin(k):
        return (z - s * k + 16) % 16

    def hops(k):
        return {1: (2, 1), 2: ()}.get(k, (1,) if k < 8 else ())

    def z_step(t, k):
        def go():
            o = origin(k)
            for q in (c, 1 - c):
                z_copy(t, o, q).wait_recv()

                def send():
                    for hop in hops(k):
                        z_copy(t, o, q, hop).start()

                if k == 7:
                    pl.when(c == t)(send)
                else:
                    send()

            g_copy(t, o).start()

        if k < 8:
            go()
        else:
            pl.when(c == t)(go)

    def wx_copy(d, p):
        q = (y + 2 * p) % 4
        to = (x + d) % 4
        return rcopy(
            cb.at[pl.ds(2 * q, 2), to],
            W.at[pl.ds(2 * q, 2), :, :, pl.ds(128 * (4 - d), 128)],
            wx_send.at[d - 1, p], wx_recv.at[d - 1, p], wide(l, to, c),
        )

    def wx_wait(d, p):
        q = (y + 2 * p) % 4
        part = W.at[pl.ds(2 * q, 2), :, :, pl.ds(128 * (4 - d), 128)]
        rcopy(part, part, wx_send.at[d - 1, p], wx_recv.at[d - 1, p], sib).wait_recv()

    def wy_copy(d, up):
        part = W.at[pl.ds(2 * y, 2), :, :, pl.ds(128 * (4 - d), 128)]
        return rcopy(
            part, part, wy_send.at[d - 1, up], wy_recv.at[d - 1, up],
            narrow(h, (y + 2 * up + 3) % 4),
        )

    def wy_wait(d, up):
        q = (y + 5 - 2 * up) % 4
        part = W.at[pl.ds(2 * q, 2), :, :, pl.ds(128 * (4 - d), 128)]
        rcopy(part, part, wy_send.at[d - 1, up], wy_recv.at[d - 1, up], sib).wait_recv()

    def w_step(d):
        wx_wait(d, 0)
        wy_copy(d, 1).start()
        wy_copy(d, 0).start()

    for t in range(2):
        z_copy(t, z, c).start()
        g0_copy(t).start()
    for t in range(2):
        g0_wait(t)
        z_copy(t, z, 1 - c).start()
    for p in range(2):
        for d in (1, 3, 2):
            wx_copy(d, p).start()

    acc[...] = jnp.zeros_like(acc)
    for i in range(3, 7):
        loads[i].wait()

    def transpose(i):
        CT[i] = cycV[i].T

    def mac(t, o):
        block = jnp.concatenate([G[t, o, 0], G[t, o, 1]], axis=1)
        acc[t, o // 8] += dot_nn(block, W[o % 8].reshape(256, 512))

    def macs(t, k):
        if k == 0:
            mac(t, z)
        elif k < 8:
            mac(t, origin(k))
            other = (z + s * k + 16) % 16
            g_copy(t, other).wait_recv()
            mac(t, other)
        else:
            far = (z + 8) % 16

            @pl.when(c != t)
            def _():
                g_copy(t, far).wait_recv()

            mac(t, far)

    def xr_copy(t, hh, d):
        return rcopy(
            XS.at[t, d - 1, hh], XR.at[t, d - 1, hh],
            xr_send.at[t, hh, d - 1], xr_recv.at[t, hh, d - 1], wide(l, (x + d) % 4, c),
        )

    def send_partials(t):
        for hh in range(2):
            for d in (2, 1, 3):
                XS[t, d - 1, hh] = acc[t, hh, :, 128 * d : 128 * d + 128].astype(BF16)
                xr_copy(t, hh, d).start()

    def z_steps(k):
        z_step(0, k)
        z_step(1, k)

    z_steps(1)
    w_step(1)
    w_step(3)
    z_steps(2)
    w_step(2)
    for i in range(4):
        transpose(i)
    z_steps(3)
    for i in range(4, 8):
        transpose(i)
    spec[...] = jnp.broadcast_to(cycrV[...], (128, 256)).T * cellV[...] + noiseS[0]
    z_steps(4)
    loads[2].wait()
    for d in (1, 3, 2):
        wx_wait(d, 1)
        wy_wait(d, 0)
        wy_wait(d, 1)
    macs(0, 0)
    macs(1, 0)
    for k in (5, 6, 7):
        z_steps(k)
        for j in ((1, 2), (3, 4), (5, 6))[k - 5]:
            macs(0, j)
            macs(1, j)
    macs(0, 7)
    z_step(0, 8)
    macs(0, 8)
    send_partials(0)
    macs(1, 7)
    z_step(1, 8)
    macs(1, 8)
    send_partials(1)

    def y_copy(t, hh, d):
        rows_of = PF.at[t, hh, y]
        return rcopy(
            rows_of, rows_of, y_send.at[t, hh, d - 1], y_recv.at[t, hh, d - 1],
            narrow(h, (y + d) % 4),
        )

    def y_wait(t, hh, d):
        rows_of = PF.at[t, hh, (y + 4 - d) % 4]
        rcopy(rows_of, rows_of, y_send.at[t, hh, d - 1], y_recv.at[t, hh, d - 1], sib).wait_recv()

    def finish_proj(t, hh):
        total = acc[t, hh, :, :128]
        for d in (1, 3, 2):
            xr_copy(t, hh, d).wait_recv()
            total = total + XR[t, d - 1, hh].astype(F32)
        PF[t, hh, y] = total.astype(BF16).reshape(4, 2, 32, 128)
        for d in (2, 1, 3):
            y_copy(t, hh, d).start()

    def pb_copy(t):
        return rcopy(PF.at[t, :, :, :, 1 - c], PB.at[t], pb_sem.at[t, 0], pb_sem.at[t, 1], sib)

    def k_copy(t):
        return rcopy(KO.at[t], KS.at[t], k_sem.at[t, 0], k_sem.at[t, 1], sib)

    def rotate(t):
        for hh in range(2):
            for d in (1, 3, 2):
                y_wait(t, hh, d)
        pb_copy(t).start()
        rot = jnp.zeros((256, 128), F32)
        for m in range(8):
            rot = rot + dot_nn(CT[m], PF[t, m // 4, m % 4].reshape(256, 128))
        KO[t] = (rot / spec[...]).astype(BF16)
        k_copy(t).start()

    for t in range(2):
        for hh in range(2):
            finish_proj(t, hh)
    rotate(0)
    coef_out[...] = KO[0]
    rotate(1)

    for t in range(2):
        pb_copy(t).wait_recv()
        k_copy(t).wait_recv()

    def rows(xx, g):
        q = dot_nt(PF[1, g, :, xx, c].reshape(128, 128), KO[0])
        q = q + dot_nt(PF[0, g, :, xx, c].reshape(128, 128), KO[1])
        q = q + dot_nt(PB[1, g, :, xx].reshape(128, 128), KS[0])
        q = q + dot_nt(PB[0, g, :, xx].reshape(128, 128), KS[1])
        return q.reshape(4, 32, 256)

    def qx_copy(g, d):
        return rcopy(
            QS.at[d - 1, g], QR.at[d - 1, g], qx_send.at[g, d - 1], qx_recv.at[g, d - 1],
            wide(l, (x + d) % 4, c),
        )

    def rz_copy(to):
        return rcopy(RS.at[to], RR.at[l], rz_send.at[to], rz_recv.at[l], wide(to, x, c))

    def rz_wait(frm):
        rcopy(
            RR.at[frm], RR.at[frm], rz_send.at[frm], rz_recv.at[frm], wide(frm, x, c)
        ).wait_recv()

    for g in range(2):
        for d in (2, 1, 3):
            QS[d - 1, g] = rows((x + d) % 4, g).astype(BF16)
            qx_copy(g, d).start()
        Q[g] = rows(x, g)
    for g in range(2):
        for d in (1, 3, 2):
            qx_copy(g, d).wait_recv()
        total = Q[g] + QR[0, g].astype(F32) + QR[2, g].astype(F32) + QR[1, g].astype(F32)
        R[4 * g : 4 * g + 4] = total
        RS[4 * g : 4 * g + 4] = total.astype(BF16)
        for to in range(4 * g, 4 * g + 4):
            @pl.when(l != to)
            def _():
                rz_copy(to).start()

    grad_out[...] = R[l]

    @pl.loop(1, 8)
    def _(k):
        rz_wait((l + k) % 8)
        grad_out[...] += RR[(l + k) % 8].astype(F32)

    def drain_gather():
        for t in range(2):
            g0_copy(t).wait_send()
            for q in range(2):
                z_copy(t, z, q).wait_send()

            for k in range(1, 8):
                o = origin(k)
                g_copy(t, o).wait_send()
                for hop in hops(k):
                    def left():
                        for q in range(2):
                            z_copy(t, o, q, hop).wait_send()

                    if k == 7:
                        pl.when(c == t)(left)
                    else:
                        left()

            @pl.when(c == t)
            def _():
                g_copy(t, (z + 8) % 16).wait_send()

            for d in range(1, 4):
                wx_copy(d, t).wait_send()
                wy_copy(d, t).wait_send()

    def drain_partials():
        for t in range(2):
            for hh in range(2):
                for d in range(1, 4):
                    xr_copy(t, hh, d).wait_send()

    def drain_proj():
        for t in range(2):
            for hh in range(2):
                for d in range(1, 4):
                    y_copy(t, hh, d).wait_send()
            pb_copy(t).wait_send()
            k_copy(t).wait_send()

    drain_gather()
    drain_partials()
    drain_proj()
    for g in range(2):
        for d in range(1, 4):
            qx_copy(g, d).wait_send()

    @pl.loop(1, 8)
    def _(k):
        rz_copy((l + k) % 8).wait_send()


def on_device(obs, cot, cell_basis, cycle_basis, cell_spectrum, cycle_spectrum, noise_var):
    vmem = pl.BlockSpec(memory_space=pltpu.VMEM)
    dma = pltpu.SemaphoreType.DMA
    return pl.pallas_call(
        kernel,
        out_shape=(
            jax.ShapeDtypeStruct((256, 128), BF16),
            jax.ShapeDtypeStruct((32, 256), F32),
        ),
        in_specs=[pl.BlockSpec(memory_space=pltpu.HBM)] * 7,
        out_specs=(vmem, vmem),
        scratch_shapes=[
            pltpu.VMEM((2, 16, 2, 256, 128), BF16),
            pltpu.VMEM((8, 2, 128, 512), BF16),
            pltpu.VMEM((2, 2, 256, 512), F32),
            pltpu.VMEM((2, 3, 2, 256, 128), BF16),
            pltpu.VMEM((2, 3, 2, 256, 128), BF16),
            pltpu.VMEM((2, 2, 4, 4, 2, 32, 128), BF16),
            pltpu.VMEM((2, 2, 4, 4, 32, 128), BF16),
            pltpu.VMEM((8, 256, 256), BF16),
            pltpu.VMEM((8, 256, 256), BF16),
            pltpu.VMEM((1, 128), F32),
            pltpu.VMEM((1, 256), F32),
            pltpu.SMEM((1,), F32),
            pltpu.VMEM((256, 128), F32),
            pltpu.VMEM((2, 256, 128), BF16),
            pltpu.VMEM((2, 256, 128), BF16),
            pltpu.VMEM((2, 4, 32, 256), F32),
            pltpu.VMEM((3, 2, 4, 32, 256), BF16),
            pltpu.VMEM((3, 2, 4, 32, 256), BF16),
            pltpu.VMEM((8, 32, 256), F32),
            pltpu.VMEM((8, 32, 256), BF16),
            pltpu.VMEM((8, 32, 256), BF16),
            dma((7,)),
            dma((2, 2)),
            dma((2, 16, 2, 2)), dma((2, 16, 2)),
            dma((2, 16)), dma((2, 16)),
            dma((3, 2)), dma((3, 2)),
            dma((3, 2)), dma((3, 2)),
            dma((2, 2, 3)), dma((2, 2, 3)),
            dma((2, 2, 3)), dma((2, 2, 3)),
            dma((2, 2)), dma((2, 2)),
            dma((2, 3)), dma((2, 3)),
            dma((8,)), dma((8,)),
        ],
        compiler_params=pltpu.CompilerParams(
            collective_id=0, has_side_effects=True, vmem_limit_bytes=60 << 20
        ),
    )(
        obs,
        cot,
        cell_basis.reshape(8, 4, 2, 128, 128),
        cycle_basis.reshape(8, 256, 256),
        cell_spectrum.reshape(1, 128),
        cycle_spectrum.reshape(1, 256),
        noise_var,
    )


def solution(mesh):
    in_specs = (
        P("narrow", "wide"),
        P("narrow", "wide"),
        P(None, "wide"),
        P(None, "narrow"),
        P("wide"),
        P("narrow"),
        P(),
    )
    out_specs = (P("narrow", "wide"), P("wide", "narrow"))
    return jax.shard_map(
        on_device, mesh=mesh, in_specs=in_specs, out_specs=out_specs, check_vma=False
    )
```

time: 95.4 us -> 89.4 us (0.937)
  Pallas kernels: 91 us -> 84.3 us
    pallas_call x1, Pallas kernels: 91 us -> 84.3 us  [on_device(): pl.pallas_call(kernel, out_shape=(jax.ShapeDtypeStruct((256, 128), BF16),...]
where the time goes in v3:
time: 89.4 us; the launch traced here: 88.4 us
  Pallas kernels  84.3 us (94%)
  local copies, waits for them, and re-layouts  2.85 us (3%)
  between operations  1.29 us (1%)
    pallas_call x1, Pallas kernels, on_device(): pl.pallas_call(kernel, out_shape=(jax.ShapeDtypeStruct((256, 128), BF16),...  84.3 us
    unnamed x2, local copies, waits for them, and re-layouts  2.85 us

profile of v3, /device:TPU:1, one launch (start us, length us, event | category | flops | bytes accessed | tf_op | source)
XLA Modules:
  0.0 88.4 jit_solution(15539722267444159019)
XLA Ops:
  1.3 84.3 %shard_map.86 = (bf16[256,128]{1,0:T(8,128)(2,1)}, f32[32,256]{1,0:T(8,128)}) custom-call(bf16[256,128]{1,0:T(8,128)(2,1)} %obs.1, bf16[256,128]{1,0:T(8,128)(2,1)} %cot.1, bf16[8,4,2,128,128]{4,3,2,1,0:T(8,128)(2,1)} %bitcast.4, bf16[8,256,256]{2,1,0:T(8,128)(2,1)} %bitcast.5, f32[1,128]{1,0:T(1,128)} %bitcast.7, f32[1,256]{1,0:T(1,128)} %bitcast.6, ...), custom_call_target="tpu_custom_call" | custom-call | tf_op jit(solution)/shard_map/pallas_call | solution.py:391
  85.5 1.5 %copy.12 = bf16[256,128]{1,0:T(8,128)(2,1)} copy(bf16[256,128]{1,0:T(8,128)(2,1)} %get-tuple-element.4) | data formatting | bytes 131072
  87.0 1.4 %copy.13 = f32[32,256]{1,0:T(8,128)} copy(f32[32,256]{1,0:T(8,128)} %get-tuple-element.5) | data formatting | bytes 65536

commit v4 on v3

--- a/solution.py
+++ b/solution.py
@@ -58,13 +58,12 @@
     for d in (2, 1, 3):
         greet(wide(l, (x + d) % 4, c))
         greet(narrow(h, (y + d) % 4))
-    greet(along_z((z - 2 * s + 16) % 16))
     greet(along_z((z - s + 16) % 16))
     greet(sib)
 
     loads = [
-        pltpu.make_async_copy(obs, G.at[0, z, c], in_sem.at[0]),
-        pltpu.make_async_copy(cot, G.at[1, z, c], in_sem.at[1]),
+        pltpu.make_async_copy(obs, G.at[z, 0, c], in_sem.at[0]),
+        pltpu.make_async_copy(cot, G.at[z, 1, c], in_sem.at[1]),
         pltpu.make_async_copy(cb.at[:, x], W.at[:, :, :, pl.ds(0, 128)], in_sem.at[2]),
         pltpu.make_async_copy(cyc, cycV, in_sem.at[3]),
         pltpu.make_async_copy(cell_row, cellV, in_sem.at[4]),
@@ -75,30 +74,30 @@
         load.start()
     loads[0].wait()
     loads[1].wait()
-    pl.semaphore_wait(bar, 9)
-
-    def z_copy(t, o, q, hop=1):
-        part = G.at[t, o, q]
-        return rcopy(
-            part, part, z_send.at[t, o, q, hop - 1], z_recv.at[t, o, q],
-            along_z((z + hop * s + 16) % 16),
+    pl.semaphore_wait(bar, 8)
+
+    def z_copy(t, o, q):
+        part = G.at[o, t, q]
+        return rcopy(
+            part, part, z_send.at[t, o, q], z_recv.at[t, o, q], along_z((z + s + 16) % 16)
         )
 
     def g0_copy(t):
-        return rcopy(G.at[t, z, c], G.at[t, z, c], g0_sem.at[t, 0], g0_sem.at[t, 1], sib)
+        return rcopy(G.at[z, t, c], G.at[z, t, c], g0_sem.at[t, 0], g0_sem.at[t, 1], sib)
 
     def g0_wait(t):
-        part = G.at[t, z, 1 - c]
+        part = G.at[z, t, 1 - c]
         rcopy(part, part, g0_sem.at[t, 0], g0_sem.at[t, 1], sib).wait_recv()
 
-    def g_copy(t, o):
-        return rcopy(G.at[t, o], G.at[t, o], g_send.at[t, o], g_recv.at[t, o], sib)
+    def g_copy(o):
+        return rcopy(G.at[o], G.at[o], g_send.at[o], g_recv.at[o], sib)
+
+    def g_far(t):
+        far = (z + 8) % 16
+        return rcopy(G.at[far, t], G.at[far, t], g_send.at[far], g_recv.at[far], sib)
 
     def origin(k):
         return (z - s * k + 16) % 16
-
-    def hops(k):
-        return {1: (2, 1), 2: ()}.get(k, (1,) if k < 8 else ())
 
     def z_step(t, k):
         def go():
@@ -107,15 +106,15 @@
                 z_copy(t, o, q).wait_recv()
 
                 def send():
-                    for hop in hops(k):
-                        z_copy(t, o, q, hop).start()
-
-                if k == 7:
+                    z_copy(t, o, q).start()
+
+                if k < 7:
+                    send()
+                elif k == 7:
                     pl.when(c == t)(send)
-                else:
-                    send()
-
-            g_copy(t, o).start()
+
+            if k == 8:
+                g_far(t).start()
 
         if k < 8:
             go()
@@ -171,7 +170,7 @@
         CT[i] = cycV[i].T
 
     def mac(t, o):
-        block = jnp.concatenate([G[t, o, 0], G[t, o, 1]], axis=1)
+        block = jnp.concatenate([G[o, t, 0], G[o, t, 1]], axis=1)
         acc[t, o // 8] += dot_nn(block, W[o % 8].reshape(256, 512))
 
     def macs(t, k):
@@ -180,14 +179,15 @@
         elif k < 8:
             mac(t, origin(k))
             other = (z + s * k + 16) % 16
-            g_copy(t, other).wait_recv()
+            if t == 0:
+                g_copy(other).wait_recv()
             mac(t, other)
         else:
             far = (z + 8) % 16
 
             @pl.when(c != t)
             def _():
-                g_copy(t, far).wait_recv()
+                g_far(t).wait_recv()
 
             mac(t, far)
 
@@ -206,6 +206,7 @@
     def z_steps(k):
         z_step(0, k)
         z_step(1, k)
+        g_copy(origin(k)).start()
 
     z_steps(1)
     w_step(1)
@@ -340,20 +341,21 @@
 
             for k in range(1, 8):
                 o = origin(k)
-                g_copy(t, o).wait_send()
-                for hop in hops(k):
-                    def left():
-                        for q in range(2):
-                            z_copy(t, o, q, hop).wait_send()
-
-                    if k == 7:
-                        pl.when(c == t)(left)
-                    else:
-                        left()
+                if t == 0:
+                    g_copy(o).wait_send()
+
+                def left():
+                    for q in range(2):
+                        z_copy(t, o, q).wait_send()
+
+                if k < 7:
+                    left()
+                else:
+                    pl.when(c == t)(left)
 
             @pl.when(c == t)
             def _():
-                g_copy(t, (z + 8) % 16).wait_send()
+                g_far(t).wait_send()
 
             for d in range(1, 4):
                 wx_copy(d, t).wait_send()
@@ -385,10 +387,15 @@
         rz_copy((l + k) % 8).wait_send()
 
 
+def hand_over(coef_in, grad_in, coef_out, grad_out):
+    coef_out[...] = coef_in[...]
+    grad_out[...] = grad_in[...]
+
+
 def on_device(obs, cot, cell_basis, cycle_basis, cell_spectrum, cycle_spectrum, noise_var):
     vmem = pl.BlockSpec(memory_space=pltpu.VMEM)
     dma = pltpu.SemaphoreType.DMA
-    return pl.pallas_call(
+    coefficients, basis_grad = pl.pallas_call(
         kernel,
         out_shape=(
             jax.ShapeDtypeStruct((256, 128), BF16),
@@ -397,7 +404,7 @@
         in_specs=[pl.BlockSpec(memory_space=pltpu.HBM)] * 7,
         out_specs=(vmem, vmem),
         scratch_shapes=[
-            pltpu.VMEM((2, 16, 2, 256, 128), BF16),
+            pltpu.VMEM((16, 2, 2, 256, 128), BF16),
             pltpu.VMEM((8, 2, 128, 512), BF16),
             pltpu.VMEM((2, 2, 256, 512), F32),
             pltpu.VMEM((2, 3, 2, 256, 128), BF16),
@@ -420,8 +427,8 @@
             pltpu.VMEM((8, 32, 256), BF16),
             dma((7,)),
             dma((2, 2)),
-            dma((2, 16, 2, 2)), dma((2, 16, 2)),
-            dma((2, 16)), dma((2, 16)),
+            dma((2, 16, 2)), dma((2, 16, 2)),
+            dma((16,)), dma((16,)),
             dma((3, 2)), dma((3, 2)),
             dma((3, 2)), dma((3, 2)),
             dma((2, 2, 3)), dma((2, 2, 3)),
@@ -442,6 +449,15 @@
         cycle_spectrum.reshape(1, 256),
         noise_var,
     )
+    return pl.pallas_call(
+        hand_over,
+        out_shape=(
+            jax.ShapeDtypeStruct((256, 128), BF16),
+            jax.ShapeDtypeStruct((32, 256), F32),
+        ),
+        in_specs=[vmem] * 2,
+        out_specs=(vmem, vmem),
+    )(coefficients, basis_grad)
 
 
 def solution(mesh):

time: 89.4 us -> 83.1 us (0.930)
  Pallas kernels: 84.3 us -> 81.3 us
  local copies, waits for them, and re-layouts: 2.85 us -> 0 us
    pallas_call x1, Pallas kernels: 84.3 us -> 79.8 us  [on_device(): pl.pallas_call(kernel, out_shape=(jax.ShapeDtypeStruct((256, 128), BF16),...]
    unnamed x2 -> x0, local copies, waits for them, and re-layouts: 2.85 us -> none
    pallas_call x0 -> x1, Pallas kernels: none -> 1.48 us  [on_device(): pl.pallas_call(hand_over, out_shape=(jax.ShapeDtypeStruct((256, 128), BF1...]
where the time goes in v4:
time: 83.1 us; the launch traced here: 82.6 us
  Pallas kernels  81.3 us (98%)
  between operations  1.29 us (2%)
    pallas_call x1, Pallas kernels, on_device(): pl.pallas_call(kernel, out_shape=(jax.ShapeDtypeStruct((256, 128), BF16),...  79.8 us

profile of v4, /device:TPU:1, one launch (start us, length us, event | category | flops | bytes accessed | tf_op | source)
XLA Modules:
  0.0 82.6 jit_solution(9781630977812011999)
XLA Ops:
  1.3 79.8 %shard_map.86 = (bf16[256,128]{1,0:T(8,128)(2,1)}, f32[32,256]{1,0:T(8,128)}) custom-call(bf16[256,128]{1,0:T(8,128)(2,1)} %obs.1, bf16[256,128]{1,0:T(8,128)(2,1)} %cot.1, bf16[8,4,2,128,128]{4,3,2,1,0:T(8,128)(2,1)} %bitcast.4, bf16[8,256,256]{2,1,0:T(8,128)(2,1)} %bitcast.5, f32[1,128]{1,0:T(1,128)} %bitcast.7, f32[1,256]{1,0:T(1,128)} %bitcast.6, ...), custom_call_target="tpu_custom_call" | custom-call | tf_op jit(solution)/shard_map/pallas_call | solution.py:398
  81.1 1.5 %shard_map.87 = (bf16[256,128]{1,0:T(8,128)(2,1)}, f32[32,256]{1,0:T(8,128)}) custom-call(bf16[256,128]{1,0:T(8,128)(2,1)} %get-tuple-element.4.coef_in, f32[32,256]{1,0:T(8,128)} %get-tuple-element.5.grad_in), custom_call_target="tpu_custom_call" | custom-call | tf_op jit(solution)/shard_map/pallas_call | solution.py:452

commit v5 on v4

--- a/solution.py
+++ b/solution.py
@@ -171,25 +171,29 @@
 
     def mac(t, o):
         block = jnp.concatenate([G[o, t, 0], G[o, t, 1]], axis=1)
-        acc[t, o // 8] += dot_nn(block, W[o % 8].reshape(256, 512))
-
-    def macs(t, k):
-        if k == 0:
-            mac(t, z)
-        elif k < 8:
-            mac(t, origin(k))
-            other = (z + s * k + 16) % 16
-            if t == 0:
-                g_copy(other).wait_recv()
-            mac(t, other)
-        else:
-            far = (z + 8) % 16
-
-            @pl.when(c != t)
-            def _():
-                g_far(t).wait_recv()
-
-            mac(t, far)
+        acc[o // 8, t] += dot_nn(block, W[o % 8].reshape(256, 512))
+
+    def mac_both(o):
+        block = jnp.concatenate(
+            [G[o, :, 0].reshape(512, 128), G[o, :, 1].reshape(512, 128)], axis=1
+        )
+        part = dot_nn(block, W[o % 8].reshape(256, 512))
+        acc[o // 8] += part.reshape(2, 256, 512)
+
+    def macs(k):
+        mac_both(origin(k))
+        other = (z + s * k + 16) % 16
+        g_copy(other).wait_recv()
+        mac_both(other)
+
+    def last_mac(t):
+        z_step(t, 8)
+
+        @pl.when(c != t)
+        def _():
+            g_far(t).wait_recv()
+
+        mac(t, (z + 8) % 16)
 
     def xr_copy(t, hh, d):
         return rcopy(
@@ -200,7 +204,7 @@
     def send_partials(t):
         for hh in range(2):
             for d in (2, 1, 3):
-                XS[t, d - 1, hh] = acc[t, hh, :, 128 * d : 128 * d + 128].astype(BF16)
+                XS[t, d - 1, hh] = acc[hh, t, :, 128 * d : 128 * d + 128].astype(BF16)
                 xr_copy(t, hh, d).start()
 
     def z_steps(k):
@@ -225,20 +229,15 @@
         wx_wait(d, 1)
         wy_wait(d, 0)
         wy_wait(d, 1)
-    macs(0, 0)
-    macs(1, 0)
+    mac_both(z)
+    macs(1)
     for k in (5, 6, 7):
         z_steps(k)
-        for j in ((1, 2), (3, 4), (5, 6))[k - 5]:
-            macs(0, j)
-            macs(1, j)
-    macs(0, 7)
-    z_step(0, 8)
-    macs(0, 8)
+        for j in ((2, 3), (4, 5), (6, 7))[k - 5]:
+            macs(j)
+    last_mac(0)
     send_partials(0)
-    macs(1, 7)
-    z_step(1, 8)
-    macs(1, 8)
+    last_mac(1)
     send_partials(1)
 
     def y_copy(t, hh, d):
@@ -253,7 +252,7 @@
         rcopy(rows_of, rows_of, y_send.at[t, hh, d - 1], y_recv.at[t, hh, d - 1], sib).wait_recv()
 
     def finish_proj(t, hh):
-        total = acc[t, hh, :, :128]
+        total = acc[hh, t, :, :128]
         for d in (1, 3, 2):
             xr_copy(t, hh, d).wait_recv()
             total = total + XR[t, d - 1, hh].astype(F32)
@@ -261,20 +260,22 @@
         for d in (2, 1, 3):
             y_copy(t, hh, d).start()
 
-    def pb_copy(t):
-        return rcopy(PF.at[t, :, :, :, 1 - c], PB.at[t], pb_sem.at[t, 0], pb_sem.at[t, 1], sib)
+    def pb_copy(t, hh):
+        return rcopy(
+            PF.at[t, hh, :, :, 1 - c], PB.at[t, hh], pb_sem.at[t, hh, 0], pb_sem.at[t, hh, 1], sib
+        )
 
     def k_copy(t):
         return rcopy(KO.at[t], KS.at[t], k_sem.at[t, 0], k_sem.at[t, 1], sib)
 
     def rotate(t):
+        rot = jnp.zeros((256, 128), F32)
         for hh in range(2):
             for d in (1, 3, 2):
                 y_wait(t, hh, d)
-        pb_copy(t).start()
-        rot = jnp.zeros((256, 128), F32)
-        for m in range(8):
-            rot = rot + dot_nn(CT[m], PF[t, m // 4, m % 4].reshape(256, 128))
+            pb_copy(t, hh).start()
+            for yy in range(4):
+                rot = rot + dot_nn(CT[4 * hh + yy], PF[t, hh, yy].reshape(256, 128))
         KO[t] = (rot / spec[...]).astype(BF16)
         k_copy(t).start()
 
@@ -285,13 +286,11 @@
     coef_out[...] = KO[0]
     rotate(1)
 
-    for t in range(2):
-        pb_copy(t).wait_recv()
-        k_copy(t).wait_recv()
-
-    def rows(xx, g):
+    def own_rows(xx, g):
         q = dot_nt(PF[1, g, :, xx, c].reshape(128, 128), KO[0])
-        q = q + dot_nt(PF[0, g, :, xx, c].reshape(128, 128), KO[1])
+        return q + dot_nt(PF[0, g, :, xx, c].reshape(128, 128), KO[1])
+
+    def all_rows(q, xx, g):
         q = q + dot_nt(PB[1, g, :, xx].reshape(128, 128), KS[0])
         q = q + dot_nt(PB[0, g, :, xx].reshape(128, 128), KS[1])
         return q.reshape(4, 32, 256)
@@ -311,10 +310,16 @@
         ).wait_recv()
 
     for g in range(2):
-        for d in (2, 1, 3):
-            QS[d - 1, g] = rows((x + d) % 4, g).astype(BF16)
+        own = [own_rows((x + d) % 4, g) for d in (2, 1, 3)]
+        if g == 0:
+            for t in range(2):
+                for hh in range(2):
+                    pb_copy(t, hh).wait_recv()
+                k_copy(t).wait_recv()
+        for q, d in zip(own, (2, 1, 3)):
+            QS[d - 1, g] = all_rows(q, (x + d) % 4, g).astype(BF16)
             qx_copy(g, d).start()
-        Q[g] = rows(x, g)
+        Q[g] = all_rows(own_rows(x, g), x, g)
     for g in range(2):
         for d in (1, 3, 2):
             qx_copy(g, d).wait_recv()
@@ -372,7 +377,8 @@
             for hh in range(2):
                 for d in range(1, 4):
                     y_copy(t, hh, d).wait_send()
-            pb_copy(t).wait_send()
+            for hh in range(2):
+                pb_copy(t, hh).wait_send()
             k_copy(t).wait_send()
 
     drain_gather()
@@ -433,7 +439,7 @@
             dma((3, 2)), dma((3, 2)),
             dma((2, 2, 3)), dma((2, 2, 3)),
             dma((2, 2, 3)), dma((2, 2, 3)),
-            dma((2, 2)), dma((2, 2)),
+            dma((2, 2, 2)), dma((2, 2)),
             dma((2, 3)), dma((2, 3)),
             dma((8,)), dma((8,)),
         ],

time: 83.1 us -> 82.9 us (level)
  no operation moved by 1% of the time
where the time goes in v5:
time: 82.9 us; the launch traced here: 82.3 us
  Pallas kernels  81.1 us (98%)
  between operations  1.29 us (2%)
    pallas_call x1, Pallas kernels, on_device(): pl.pallas_call(kernel, out_shape=(jax.ShapeDtypeStruct((256, 128), BF16),...  79.6 us

profile of v5, /device:TPU:1, one launch (start us, length us, event | category | flops | bytes accessed | tf_op | source)
XLA Modules:
  0.0 82.3 jit_solution(8359282231318256709)
XLA Ops:
  1.3 79.6 %shard_map.86 = (bf16[256,128]{1,0:T(8,128)(2,1)}, f32[32,256]{1,0:T(8,128)}) custom-call(bf16[256,128]{1,0:T(8,128)(2,1)} %obs.1, bf16[256,128]{1,0:T(8,128)(2,1)} %cot.1, bf16[8,4,2,128,128]{4,3,2,1,0:T(8,128)(2,1)} %bitcast.4, bf16[8,256,256]{2,1,0:T(8,128)(2,1)} %bitcast.5, f32[1,128]{1,0:T(1,128)} %bitcast.7, f32[1,256]{1,0:T(1,128)} %bitcast.6, ...), custom_call_target="tpu_custom_call" | custom-call | tf_op jit(solution)/shard_map/pallas_call | solution.py:404
  80.9 1.5 %shard_map.87 = (bf16[256,128]{1,0:T(8,128)(2,1)}, f32[32,256]{1,0:T(8,128)}) custom-call(bf16[256,128]{1,0:T(8,128)(2,1)} %get-tuple-element.4.coef_in, f32[32,256]{1,0:T(8,128)} %get-tuple-element.5.grad_in), custom_call_target="tpu_custom_call" | custom-call | tf_op jit(solution)/shard_map/pallas_call | solution.py:458

commit v6 on v5

--- a/solution.py
+++ b/solution.py
@@ -201,11 +201,10 @@
             xr_send.at[t, hh, d - 1], xr_recv.at[t, hh, d - 1], wide(l, (x + d) % 4, c),
         )
 
-    def send_partials(t):
-        for hh in range(2):
-            for d in (2, 1, 3):
-                XS[t, d - 1, hh] = acc[hh, t, :, 128 * d : 128 * d + 128].astype(BF16)
-                xr_copy(t, hh, d).start()
+    def send_partials(t, hh):
+        for d in (2, 1, 3):
+            XS[t, d - 1, hh] = acc[hh, t, :, 128 * d : 128 * d + 128].astype(BF16)
+            xr_copy(t, hh, d).start()
 
     def z_steps(k):
         z_step(0, k)
@@ -235,10 +234,11 @@
         z_steps(k)
         for j in ((2, 3), (4, 5), (6, 7))[k - 5]:
             macs(j)
-    last_mac(0)
-    send_partials(0)
-    last_mac(1)
-    send_partials(1)
+    for t in range(2):
+        send_partials(t, h)
+    for t in range(2):
+        last_mac(t)
+        send_partials(t, 1 - h)
 
     def y_copy(t, hh, d):
         rows_of = PF.at[t, hh, y]
@@ -270,7 +270,7 @@
 
     def rotate(t):
         rot = jnp.zeros((256, 128), F32)
-        for hh in range(2):
+        for hh in (h, 1 - h):
             for d in (1, 3, 2):
                 y_wait(t, hh, d)
             pb_copy(t, hh).start()
@@ -279,8 +279,8 @@
         KO[t] = (rot / spec[...]).astype(BF16)
         k_copy(t).start()
 
-    for t in range(2):
-        for hh in range(2):
+    for hh in (h, 1 - h):
+        for t in range(2):
             finish_proj(t, hh)
     rotate(0)
     coef_out[...] = KO[0]

time: 82.9 us -> 81.6 us (0.984); the launches traced: 82.3 us -> 79.9 us
  Pallas kernels: 81.1 us -> 78.7 us
    pallas_call x1, Pallas kernels: 79.6 us -> 77.2 us  [on_device(): pl.pallas_call(kernel, out_shape=(jax.ShapeDtypeStruct((256, 128), BF16),...]
where the time goes in v6:
time: 81.6 us; the launch traced here: 79.9 us
  Pallas kernels  78.7 us (96%)
  between operations  1.29 us (2%)
    pallas_call x1, Pallas kernels, on_device(): pl.pallas_call(kernel, out_shape=(jax.ShapeDtypeStruct((256, 128), BF16),...  77.2 us

profile of v6, /device:TPU:1, one launch (start us, length us, event | category | flops | bytes accessed | tf_op | source)
XLA Modules:
  0.0 79.9 jit_solution(3113301608648256446)
XLA Ops:
  1.3 77.2 %shard_map.86 = (bf16[256,128]{1,0:T(8,128)(2,1)}, f32[32,256]{1,0:T(8,128)}) custom-call(bf16[256,128]{1,0:T(8,128)(2,1)} %obs.1, bf16[256,128]{1,0:T(8,128)(2,1)} %cot.1, bf16[8,4,2,128,128]{4,3,2,1,0:T(8,128)(2,1)} %bitcast.4, bf16[8,256,256]{2,1,0:T(8,128)(2,1)} %bitcast.5, f32[1,128]{1,0:T(1,128)} %bitcast.7, f32[1,256]{1,0:T(1,128)} %bitcast.6, ...), custom_call_target="tpu_custom_call" | custom-call | tf_op jit(solution)/shard_map/pallas_call | solution.py:404
  78.5 1.5 %shard_map.87 = (bf16[256,128]{1,0:T(8,128)(2,1)}, f32[32,256]{1,0:T(8,128)}) custom-call(bf16[256,128]{1,0:T(8,128)(2,1)} %get-tuple-element.4.coef_in, f32[32,256]{1,0:T(8,128)} %get-tuple-element.5.grad_in), custom_call_target="tpu_custom_call" | custom-call | tf_op jit(solution)/shard_map/pallas_call | solution.py:458

commit v7 on v6

--- a/solution.py
+++ b/solution.py
@@ -309,9 +309,10 @@
             RR.at[frm], RR.at[frm], rz_send.at[frm], rz_recv.at[frm], wide(frm, x, c)
         ).wait_recv()
 
-    for g in range(2):
+    halves = (1 - l // 4, l // 4)
+    for g in halves:
         own = [own_rows((x + d) % 4, g) for d in (2, 1, 3)]
-        if g == 0:
+        if g is halves[0]:
             for t in range(2):
                 for hh in range(2):
                     pb_copy(t, hh).wait_recv()
@@ -320,13 +321,13 @@
             QS[d - 1, g] = all_rows(q, (x + d) % 4, g).astype(BF16)
             qx_copy(g, d).start()
         Q[g] = all_rows(own_rows(x, g), x, g)
-    for g in range(2):
+    for g in halves:
         for d in (1, 3, 2):
             qx_copy(g, d).wait_recv()
         total = Q[g] + QR[0, g].astype(F32) + QR[2, g].astype(F32) + QR[1, g].astype(F32)
-        R[4 * g : 4 * g + 4] = total
-        RS[4 * g : 4 * g + 4] = total.astype(BF16)
-        for to in range(4 * g, 4 * g + 4):
+        R[pl.ds(4 * g, 4)] = total
+        RS[pl.ds(4 * g, 4)] = total.astype(BF16)
+        for to in [4 * g + i for i in range(4)]:
             @pl.when(l != to)
             def _():
                 rz_copy(to).start()

time: 81.6 us -> 81.7 us (level); the launches traced: 79.9 us -> 81.5 us
  Pallas kernels: 78.7 us -> 80.2 us
    pallas_call x1, Pallas kernels: 77.2 us -> 78.7 us  [on_device(): pl.pallas_call(kernel, out_shape=(jax.ShapeDtypeStruct((256, 128), BF16),...]
where the time goes in v7:
time: 81.7 us; the launch traced here: 81.5 us
  Pallas kernels  80.2 us (98%)
  between operations  1.29 us (2%)
    pallas_call x1, Pallas kernels, on_device(): pl.pallas_call(kernel, out_shape=(jax.ShapeDtypeStruct((256, 128), BF16),...  78.7 us

profile of v7, /device:TPU:1, one launch (start us, length us, event | category | flops | bytes accessed | tf_op | source)
XLA Modules:
  0.0 81.5 jit_solution(13415794974754868968)
XLA Ops:
  1.3 78.7 %shard_map.86 = (bf16[256,128]{1,0:T(8,128)(2,1)}, f32[32,256]{1,0:T(8,128)}) custom-call(bf16[256,128]{1,0:T(8,128)(2,1)} %obs.1, bf16[256,128]{1,0:T(8,128)(2,1)} %cot.1, bf16[8,4,2,128,128]{4,3,2,1,0:T(8,128)(2,1)} %bitcast.4, bf16[8,256,256]{2,1,0:T(8,128)(2,1)} %bitcast.5, f32[1,128]{1,0:T(1,128)} %bitcast.7, f32[1,256]{1,0:T(1,128)} %bitcast.6, ...), custom_call_target="tpu_custom_call" | custom-call | tf_op jit(solution)/shard_map/pallas_call | solution.py:405
  80.0 1.5 %shard_map.87 = (bf16[256,128]{1,0:T(8,128)(2,1)}, f32[32,256]{1,0:T(8,128)}) custom-call(bf16[256,128]{1,0:T(8,128)(2,1)} %get-tuple-element.4.coef_in, f32[32,256]{1,0:T(8,128)} %get-tuple-element.5.grad_in), custom_call_target="tpu_custom_call" | custom-call | tf_op jit(solution)/shard_map/pallas_call | solution.py:459
